TPU v7x, 256 devices: a whole 4x4x8 slice. The times are simulated.
256 devices in a mesh: ep: 64 (over x_hi, y, z), et: 4 (over x_lo, core).
Axes of the slice: x: 4 (x_hi: 2, x_lo: 2; x = x_hi * 2 + x_lo), y: 4, z: 8, core: 2. Of those that a mesh axis runs over, the one named last changes fastest.
Arguments:
- tokens: bfloat16 [8192, 3584], P('ep', 'et'), may hold values from -6 to 6
- slot_ids: int32 [8192, 8], P('ep'), may hold values from 0 to 63, all different within a row; in each aligned block of 128 rows (0 to 127, 128 to 255, ...) at most 20 rows name the same one
- gate_weights: float32 [8192, 8], P('ep'), may hold values from 0.1 to 1
- old_expert: int32 [64], replicated, may hold values from 0 to 55, as said below
- new_expert: int32 [64], replicated, may hold values from 0 to 55, as said below
- gate_proj: bfloat16 [64, 3584, 1024], P(None, 'ep', 'et'), may hold values from -0.09375 to 0.09375
- up_proj: bfloat16 [64, 3584, 1024], P(None, 'ep', 'et'), may hold values from -0.09375 to 0.09375
- down_proj: bfloat16 [64, 3584, 1024], P(None, 'ep', 'et'), may hold values from -0.1875 to 0.1875
Outputs:
- layer_out: bfloat16 [8192, 3584], P('ep', 'et')
Inputs may be any that keep to these rules, and one draw needn't show every extreme that they name: `slot_ids`: each row names 8 different slots. The rows of one index of ep name no slot more than 20 times, and in every draw some slot exactly 20 times on some index. `old_expert`: names every expert 0 to 55 once or twice; 8 of them twice. `new_expert`: names every expert 0 to 55 once or twice; 8 of them twice.
All inputs are finite; a program needn't handle non-finite values.
Results may differ from a plain program's by a relative error of at most 0.015.
Values may be sent and summed in bfloat16 or wider, within the bound.
A program may use at most 128 MiB of HBM per device.

v0:
```python
import jax
import jax.numpy as jnp
from jax import lax
from jax.sharding import PartitionSpec as P


def gather_rows(source_rows, row_table, slot_total, capacity):
    padded = jnp.concatenate(
        [source_rows, jnp.zeros((1, source_rows.shape[1]), source_rows.dtype)], axis=0
    )
    return jnp.take(padded, row_table, axis=0).reshape(slot_total, capacity, source_rows.shape[1])


def combine_rows(returned, target, gate_flat, tok_rows, top_count):
    flat_rows = returned.reshape(-1, returned.shape[-1])
    picked = jnp.take(flat_rows, target, axis=0).astype(jnp.float32)
    scaled = picked * gate_flat[:, None]
    return jnp.sum(scaled.reshape(tok_rows, top_count, -1), axis=1)


def per_device(
    tokens, slot_ids, gate_weights, old_expert, new_expert, gate_proj, up_proj, down_proj
):
    slot_total = lax.axis_size("ep")
    tok_rows = tokens.shape[0]
    top_count = slot_ids.shape[1]
    capacity = min(tok_rows, (tok_rows * top_count * 5 + 4 * slot_total - 1) // (4 * slot_total))
    slot_index = jnp.arange(slot_total, dtype=jnp.int32)
    holders = new_expert[:, None] == old_expert[None, :]
    source = jnp.min(jnp.where(holders, slot_index[None, :], slot_total), axis=1)
    chosen_slabs = (
        jnp.take(gate_proj, source, axis=0),
        jnp.take(up_proj, source, axis=0),
        jnp.take(down_proj, source, axis=0),
    )
    moved = (
        lax.all_to_all(chosen_slabs[0], "ep", split_axis=0, concat_axis=0, tiled=True),
        lax.all_to_all(chosen_slabs[1], "ep", split_axis=0, concat_axis=0, tiled=True),
        lax.all_to_all(chosen_slabs[2], "ep", split_axis=0, concat_axis=0, tiled=True),
    )
    gate_slab, up_slab, down_slab = (
        moved_slab.reshape(-1, moved_slab.shape[-1]) for moved_slab in moved
    )
    flat_slot = slot_ids.reshape(-1)
    onehot = (flat_slot[:, None] == slot_index[None, :]).astype(jnp.int32)
    before = jnp.cumsum(onehot, axis=0) - onehot
    position = jnp.sum(before * onehot, axis=1)
    target = flat_slot * capacity + position
    pair_row = jnp.arange(flat_slot.shape[0], dtype=jnp.int32) // top_count
    row_table = jnp.full((slot_total * capacity,), tok_rows, jnp.int32).at[target].set(pair_row)
    full_rows = lax.all_gather(tokens, "et", axis=1, tiled=True)
    arrived = lax.all_to_all(
        gather_rows(full_rows, row_table, slot_total, capacity),
        "ep",
        split_axis=0,
        concat_axis=0,
        tiled=True,
    )
    rows_in = arrived.reshape(-1, arrived.shape[-1])
    gate_part = jnp.dot(rows_in, gate_slab, preferred_element_type=jnp.float32)
    up_part = jnp.dot(rows_in, up_slab, preferred_element_type=jnp.float32)
    hidden = (jax.nn.silu(gate_part) * up_part).astype(jnp.bfloat16)
    partial_value = lax.dot_general(
        hidden, down_slab, (((1,), (1,)), ((), ())), preferred_element_type=jnp.float32
    )
    gate_flat = gate_weights.reshape(-1)
    expert_out = lax.psum_scatter(
        partial_value.astype(jnp.bfloat16), "et", scatter_dimension=1, tiled=True
    ).astype(jnp.float32)
    returned = lax.all_to_all(
        expert_out.reshape(slot_total, capacity, -1).astype(jnp.bfloat16),
        "ep",
        split_axis=0,
        concat_axis=0,
        tiled=True,
    ).astype(jnp.float32)
    layer_out = combine_rows(returned, target, gate_flat, tok_rows, top_count)
    return layer_out.astype(jnp.bfloat16)


def solution(mesh):
    placed = (
        P("ep", "et"),
        P("ep", None),
        P("ep", None),
        P(),
        P(),
        P(None, "ep", "et"),
        P(None, "ep", "et"),
        P(None, "ep", "et"),
    )
    return jax.shard_map(
        per_device, mesh=mesh, in_specs=placed, out_specs=P("ep", "et"), check_vma=False
    )
```

profile of v0, /device:TPU:56, one launch (start us, length us, event | category | flops | bytes accessed | tf_op | source)
XLA Modules:
  0.0 690.3 jit_solution(6976815458242322432)
XLA Ops:
  6.5 1.0 select_reduce_fusion
  7.6 0.5 copy-done
  8.1 1.9 gather_fusion.2
  10.0 3.6 gather_fusion.3
  13.6 1.9 gather_fusion.4
  15.5 5.1 broadcast_select_fusion.3
  20.6 61.0 %all_to_all.25 = bf16[64,56,256]{2,1,0:T(8,128)(2,1)} all-to-all(bf16[64,56,256]{2,1,0:T(8,128)(2,1)S(1)} %get-tuple-element.6), channel_id=1, replica_groups=mesh['ep'=64,'et'=4] {'ep'}, dimensions={0} | all-to-all | bytes 3670016 | tf_op jit(solution)/shard_map/all_to_all | solution.py:37
  81.6 6.4 all-to-all-start.2
  88.4 18.0 %reduce-window.6 = s32[64,8,128]{2,1,0:T(8,128)S(1)} reduce-window(s32[64,8,128]{2,1,0:T(8,128)S(1)} %fusion.7, s32[]{:T(128)} %constant.47.clone.1), window={size=1x1x128 pad=0_0x0_0x127_0}, to_apply=%region_0.1 | reduce-window | flops 8323072 | bytes 524292 | tf_op jit(solution)/shard_map/reduce-window
  106.5 0.1 copy.31
  107.0 12.2 %all_gather.3 = bf16[128,3584]{1,0:T(8,128)(2,1)S(1)} all-gather(bf16[128,896]{1,0:T(8,128)(2,1)S(1)} %copy-done.4), channel_id=1, replica_groups=mesh['ep'=64,'et'=4] {'et'}, dimensions={1}, use_global_device_ids=true | all-gather | bytes 1146880 | tf_op jit(solution)/shard_map/all_gather | solution.py:51
  119.5 4.3 scatter_custom_fusion
  123.8 7.9 %gather_fusion = bf16[1280,3584]{1,0:T(8,128)(2,1)} fusion(bf16[129,3584]{1,0:T(8,128)(2,1)S(1)} %concatenate.3, s32[2048]{0:T(1024)S(1)} %pad_clamp_fusion), kind=kCustom, calls=%fused_computation.3 | custom fusion | bytes 18355200 | tf_op jit(solution)/shard_map/jit(_take)/gather | solution.py:11
  131.8 13.1 %gather.16 = bf16[64,20,3584]{2,1,0:T(8,128)(2,1)} reshape(bf16[1280,3584]{1,0:T(8,128)(2,1)} %gather_fusion) | data formatting | bytes 18350080 | tf_op jit(solution)/shard_map/jit(_take)/gather | solution.py:11
  145.0 9.8 %broadcast_select_fusion = bf16[64,20,3584]{2,1,0:T(8,128)(2,1)} fusion(bf16[64,20,3584]{2,1,0:T(8,128)(2,1)} %gather.16, pred[64,20]{1,0:T(8,128)(4,1)S(1)} %broadcast_in_dim.56), kind=kLoop, calls=%fused_computation.7 | loop fusion | flops 4587520 | bytes 18351360 | tf_op jit(solution)/shard_map/jit(_take)/select_n | solution.py:11
  154.9 258.5 %all_to_all.26 = bf16[64,20,3584]{2,1,0:T(8,128)(2,1)} all-to-all(bf16[64,20,3584]{2,1,0:T(8,128)(2,1)} %broadcast_select_fusion), channel_id=1, replica_groups=mesh['ep'=64,'et'=4] {'ep'}, dimensions={0} | all-to-all | bytes 18350080 | tf_op jit(solution)/shard_map/all_to_all | solution.py:52
  413.3 6.3 all-to-all-start.3
  419.6 0.2 reduce-scatter.4.cloned.1.call-start
  419.9 13.3 %reshape.109 = bf16[1280,3584]{1,0:T(8,128)(2,1)} reshape(bf16[64,20,3584]{2,1,0:T(8,128)(2,1)} %all_to_all.26) | data formatting | bytes 18350080 | tf_op jit(solution)/shard_map/reshape | solution.py:59
  433.2 6.2 fusion.14
  439.4 26.8 %all-to-all-done.3 = bf16[64,56,256]{2,1,0:T(8,128)(2,1)} async-done(((bf16[64,56,256]{2,1,0:T(8,128)(2,1)}), bf16[64,56,256]{2,1,0:T(8,128)(2,1)}, u32[]{:S(2)}, u32[]{:S(2)}) %all-to-all-start.3) | async-done | bytes 1835040 | tf_op jit(solution)/shard_map/all_to_all | solution.py:39
  466.3 15.3 %convolution_convert_fusion = bf16[1280,3584]{1,0:T(8,128)(2,1)} fusion(bf16[3584,256]{1,0:T(8,128)(2,1)} %bitcast.6, bf16[1280,3584]{1,0:T(8,128)(2,1)} %reshape.109, bf16[3584,256]{1,0:T(8,128)(2,1)} %bitcast.5, f32[1280,256]{1,0:T(8,128)S(1)} %fusion.14), kind=kOutput, calls=%fused_computation.6 | convolution fusion | flops 4704174080 | bytes 23330816 | tf_op jit(solution)/shard_map/dot_general | solution.py:63
  481.6 12.7 %copy.37 = bf16[1280,3584]{0,1:T(8,128)(2,1)} copy(bf16[1280,3584]{1,0:T(8,128)(2,1)} %convolution_convert_fusion) | data formatting | bytes 18350080
  494.3 82.6 %reduce-scatter.4.cloned.1.call-done = bf16[896,1280]{1,0:T(8,128)(2,1)} async-done(((bf16[3584,1280]{1,0:T(8,128)(2,1)}), bf16[896,1280]{1,0:T(8,128)(2,1)}) %reduce-scatter.4.cloned.1.call-update) | async-done | bytes 2293776
  576.9 4.3 copy.38
  581.3 4.7 convert_element_type.26
  586.0 12.9 %all-to-all-start.4 = ((bf16[64,20,896]{2,1,0:T(8,128)(2,1)}), bf16[64,20,896]{2,1,0:T(8,128)(2,1)}, u32[]{:S(2)}, u32[]{:S(2)}) async-start(bf16[64,20,896]{2,1,0:T(8,128)(2,1)} %convert_element_type.26), calls=%async_computation.4 | async-start | bytes 5505024 | tf_op jit(solution)/shard_map/all_to_all | solution.py:70
  599.0 0.1 copy.34
  599.3 66.7 %all-to-all-done.4 = bf16[64,20,896]{2,1,0:T(8,128)(2,1)} async-done(((bf16[64,20,896]{2,1,0:T(8,128)(2,1)}), bf16[64,20,896]{2,1,0:T(8,128)(2,1)}, u32[]{:S(2)}, u32[]{:S(2)}) %all-to-all-start.4) | async-done | bytes 2293792 | tf_op jit(solution)/shard_map/all_to_all | solution.py:70
  665.9 5.0 reshape.116
  670.9 8.5 %gather_fusion.1 = f32[1024,896]{1,0:T(8,128)} fusion(f32[1280,896]{1,0:T(8,128)} %reshape.116, s32[1024]{0:T(1024)S(1)} %broadcast_clamp_fusion), kind=kCustom, calls=%fused_computation.4 | custom fusion | bytes 7344128 | tf_op jit(solution)/shard_map/jit(_take)/gather | solution.py:16
  679.4 4.0 fusion.1
  (43 shorter events, 1.5 us)
Async XLA Ops:
  6.5 1.5 copy-start
  10.0 3.6 copy-start.3
  81.6 6.4 copy-start.5
  81.6 73.3 %all-to-all-start.2 = ((bf16[64,56,256]{2,1,0:T(8,128)(2,1)}), bf16[64,56,256]{2,1,0:T(8,128)(2,1)}, u32[]{:S(2)}, u32[]{:S(2)}) async-start(bf16[64,56,256]{2,1,0:T(8,128)(2,1)} %get-tuple-element.7), calls=%async_computation.2 | async-start | bytes 3670016 | tf_op jit(solution)/shard_map/all_to_all | solution.py:38
  88.0 19.0 %copy-start.4 = (bf16[128,896]{1,0:T(8,128)(2,1)S(1)}, bf16[128,896]{1,0:T(8,128)(2,1)}, u32[]{:S(2)}) copy-start(bf16[128,896]{1,0:T(8,128)(2,1)} %param.10) | copy-start | bytes 688132
  413.3 52.9 %all-to-all-start.3 = ((bf16[64,56,256]{2,1,0:T(8,128)(2,1)}), bf16[64,56,256]{2,1,0:T(8,128)(2,1)}, u32[]{:S(2)}, u32[]{:S(2)}) async-start(bf16[64,56,256]{2,1,0:T(8,128)(2,1)} %get-tuple-element.8), calls=%async_computation.3 | async-start | bytes 3670016 | tf_op jit(solution)/shard_map/all_to_all | solution.py:39
  419.6 13.6 %copy-start.2 = (bf16[64,56,256]{2,1,0:T(8,128)(2,1)S(1)}, bf16[64,56,256]{2,1,0:T(8,128)(2,1)}, u32[]{:S(2)}) copy-start(bf16[64,56,256]{2,1,0:T(8,128)(2,1)} %all_to_all.25) | copy-start | bytes 5505028
  419.6 157.3 %reduce-scatter.4.cloned.1.call-start = ((), (), s32[]{:S(2)}) async-start(), calls=%async_computation.6 | async-start | bytes 11468800
  586.0 13.2 %copy-start.6 = (f32[128,8]{0,1:T(8,128)S(1)}, f32[128,8]{0,1:T(8,128)}, u32[]{:S(2)}) copy-start(f32[128,8]{0,1:T(8,128)} %param.12) | copy-start | bytes 12292
  586.0 80.0 %all-to-all-start.4 = ((bf16[64,20,896]{2,1,0:T(8,128)(2,1)}), bf16[64,20,896]{2,1,0:T(8,128)(2,1)}, u32[]{:S(2)}, u32[]{:S(2)}) async-start(bf16[64,20,896]{2,1,0:T(8,128)(2,1)} %convert_element_type.26), calls=%async_computation.4 | async-start | bytes 5505024 | tf_op jit(solution)/shard_map/all_to_all | solution.py:70
  670.9 12.5 %copy-start.1 = (bf16[64,56,256]{2,1,0:T(8,128)(2,1)S(1)}, bf16[64,56,256]{2,1,0:T(8,128)(2,1)}, u32[]{:S(2)}) copy-start(bf16[64,56,256]{2,1,0:T(8,128)(2,1)} %param.15) | copy-start | bytes 5505028
Sparse Core Ops, SparseCore 0:
  494.4 82.4 reduce-scatter.3
where the time goes:
time: 692 us; the launch traced here: 690 us
  blocking collectives  332 us (48%)
  waiting for transfers between devices  176 us (25%)
  local copies, waits for them, and re-layouts  83.3 us (12%)
  other arithmetic  38.2 us (6%)
  starting transfers between devices  25.8 us (4%)
  matrix products  21.5 us (3%)
  between operations  13.6 us (2%)
    all_to_all x1, blocking collectives, per_device(): lax.all_to_all(gather_rows(full_rows, row_table, slot_total, capacity), '...  258 us
    unnamed x2, waiting for transfers between devices  82.6 us
    all_to_all x1, waiting for transfers between devices, per_device(): lax.all_to_all(expert_out.reshape(slot_total, capacity, -1).astype(jnp.bf...  66.7 us
    all_to_all x1, blocking collectives, per_device(): lax.all_to_all(chosen_slabs[0], 'ep', split_axis=0, concat_axis=0, tiled=...  61 us
    all_to_all x1, waiting for transfers between devices, per_device(): lax.all_to_all(chosen_slabs[2], 'ep', split_axis=0, concat_axis=0, tiled=...  26.8 us
    gather x2, local copies, waits for them, and re-layouts, gather_rows(): jnp.take(padded, row_table, axis=0)  21.1 us
    another operation x3, other arithmetic  18.2 us
    unnamed x18, local copies, waits for them, and re-layouts  17.8 us
  transfers between devices with their start and end apart: 4, of which 3 were waited for; matrix products, arithmetic and copies ran while one was open for 11% of the time, Pallas kernels for 0%

commit v1 on v0

v1 whole, which is shorter than its diff:
```python
import functools

import jax
import jax.numpy as jnp
from jax import lax
from jax.experimental import pallas as pl
from jax.experimental.pallas import tpu as pltpu
from jax.sharding import PartitionSpec as P

MESH = pl.DeviceIdType.MESH
NZ = 8
F32 = jnp.float32
BF16 = jnp.bfloat16


def layer_kernel(
    cap,
    source_ref, tokens_hbm, slot_t_ref, gate_t_ref, gate_hbm, up_hbm, down_hbm, out_ref,
    stage_gate, stage_up, stage_down, wsend, gu_recv, down_recv, idx_send, idx_recv, tok_all, pick, combine, row_send, rows_in,
    part_send, part_recv, own, hid, out_send, ret, zsend, zrecv,
    load_sem, wsend_sem, wrecv_sem, self_sem, tok_send_sem, tok_recv_sem, idx_send_sem, idx_recv_sem,
    row_send_sem, row_recv_sem, fwd_send_sem, fwd_recv_sem, part_send_sem, part_recv_sem,
    hid_send_sem, hid_recv_sem, out_send_sem, ret_recv_sem, z_send_sem, z_recv_sem,
):
    n_ep = stage_gate.shape[0]
    n_xy = n_ep // NZ
    tok = tok_all.shape[1]
    width = tok_all.shape[2]
    line_rows = NZ * cap
    n_rows = n_xy * line_rows
    ep = lax.axis_index("ep")
    et = lax.axis_index("et")
    me_xy, me_z = ep // NZ, ep % NZ
    h, c = et // 2, et % 2
    half = ep // (n_ep // 2)
    quarter = ep // (n_ep // 4)
    gu_et = half * 2 + c
    weights_hbm = (gate_hbm, up_hbm, down_hbm)
    stage = (stage_gate, stage_up, stage_down)

    loads = [
        pltpu.make_async_copy(weights_hbm[k], stage[k], load_sem.at[k]) for k in range(3)
    ]
    token_load = pltpu.make_async_copy(tokens_hbm, tok_all.at[me_z], load_sem.at[3])
    token_load.start()
    for load in loads:
        load.start()

    barrier = pltpu.get_barrier_semaphore()

    def greet(other_ep, other_et):
        pl.semaphore_signal(barrier, inc=1, device_id=(other_ep, other_et), device_id_type=MESH)

    @pl.loop(0, n_ep)
    def _(k):
        other_ep, other_et = h * (n_ep // 2) + k // 2, (k % 2) * 2 + c

        @pl.when(jnp.logical_or(other_ep != ep, other_et != et))
        def _():
            greet(other_ep, other_et)

    @pl.loop(0, n_ep)
    def _(k):
        other_ep, other_et = et * (n_ep // 4) + k // 4, k % 4

        @pl.when(jnp.logical_or(other_ep != ep, other_et != et))
        def _():
            greet(other_ep, other_et)

    for d in range(1, NZ):
        greet(me_xy * NZ + (me_z + d) % NZ, et)
    for d in range(1, n_xy):
        greet(((me_xy + d) % n_xy) * NZ + me_z, et)
    for d in range(1, 4):
        greet(ep, (et + d) % 4)

    row = lax.broadcasted_iota(jnp.int32, (n_ep, tok), 0)
    row_slot = (row % n_xy) * NZ + row // n_xy
    named = jnp.zeros((n_ep, tok), F32)
    weight = jnp.zeros((n_ep, tok), F32)
    for k in range(slot_t_ref.shape[0]):
        hit = slot_t_ref[k : k + 1, :] == row_slot
        named = jnp.where(hit, 1.0, named)
        weight = jnp.where(hit, gate_t_ref[k : k + 1, :], weight)
    earlier = (
        lax.broadcasted_iota(jnp.int32, (tok, tok), 0) < lax.broadcasted_iota(jnp.int32, (tok, tok), 1)
    )
    place = jnp.dot(
        named.astype(BF16), jnp.where(earlier, 1.0, 0.0).astype(BF16), preferred_element_type=F32
    )
    place = jnp.where(named > 0.5, place, -100000.0)
    for z in range(NZ):
        idx_send[z, 0:n_xy, :] = place[z * n_xy : (z + 1) * n_xy]
        idx_send[z, n_xy : 2 * n_xy, :] = weight[z * n_xy : (z + 1) * n_xy]
    idx_recv[me_z] = idx_send[me_z]
    token_load.wait()

    same = jnp.where(gu_et == et, 1, 0)
    same_down = jnp.where(quarter == et, 1, 0)
    pl.semaphore_wait(barrier, 2 * n_ep - same - same_down + (NZ - 1) + (n_xy - 1) + 3)

    def token_copy(d):
        peer = me_xy * NZ + (me_z + d) % NZ
        return pltpu.make_async_remote_copy(
            tok_all.at[me_z], tok_all.at[me_z], tok_send_sem.at[d], tok_recv_sem.at[d],
            device_id=(peer, et), device_id_type=MESH,
        )

    def index_copy(d):
        peer_z = (me_z + d) % NZ
        return pltpu.make_async_remote_copy(
            idx_send.at[peer_z], idx_recv.at[me_z], idx_send_sem.at[d], idx_recv_sem.at[d],
            device_id=(me_xy * NZ + peer_z, et), device_id_type=MESH,
        )

    for d in range(1, NZ):
        index_copy(d).start()
        token_copy(d).start()

    def weight_target(k):
        if k < 2:
            return gu_et, gu_recv.at[k, et // 2, ep % (n_ep // 2)]
        return quarter, down_recv.at[et, ep % (n_ep // 4)]

    def send_weights(k):
        target_et, target = weight_target(k)

        @pl.loop(0, n_ep)
        def _(d):
            slot = (ep + d) % n_ep
            wsend[k, slot] = stage[k][source_ref[slot]]

            @pl.when(jnp.logical_or(slot != ep, target_et != et))
            def _():
                pltpu.make_async_remote_copy(
                    wsend.at[k, slot], target, wsend_sem.at[k], wrecv_sem.at[k],
                    device_id=(slot, target_et), device_id_type=MESH,
                ).start()

            @pl.when(jnp.logical_and(slot == ep, target_et == et))
            def _():
                pltpu.make_async_copy(wsend.at[k, slot], target, wrecv_sem.at[k]).start()

    def wait_weights(k):
        landed = gu_recv.at[k] if k < 2 else down_recv
        pltpu.make_async_copy(landed, landed, wrecv_sem.at[k]).wait()

    def wait_weights_sent(k):
        target_et, target = weight_target(k)

        @pl.loop(0, n_ep)
        def _(slot):
            @pl.when(jnp.logical_or(slot != ep, target_et != et))
            def _():
                pltpu.make_async_remote_copy(
                    wsend.at[k, slot], target, wsend_sem.at[k], wrecv_sem.at[k],
                    device_id=(slot, target_et), device_id_type=MESH,
                ).wait_send()

    loads[0].wait()
    send_weights(0)

    for d in range(1, NZ):
        index_copy(d).wait_recv()
        token_copy(d).wait_recv()
    line_row = lax.broadcasted_iota(jnp.int32, (line_rows, tok), 0).astype(F32)

    def row_copy(d):
        peer_xy = (me_xy + d) % n_xy
        return pltpu.make_async_remote_copy(
            row_send.at[peer_xy], rows_in.at[c, me_xy], row_send_sem.at[d], row_recv_sem.at[d],
            device_id=(peer_xy * NZ + me_z, et), device_id_type=MESH,
        )

    for d in range(1, n_xy + 1):
        j = (me_xy + d) % n_xy
        for z in range(NZ):
            line = idx_recv[z, pl.ds(j, 1), :] + float(z * cap)
            pick[:, z * tok : (z + 1) * tok] = jnp.where(line == line_row, 1.0, 0.0).astype(BF16)
        rows = jnp.dot(
            pick[...], tok_all[...].reshape(NZ * tok, width), preferred_element_type=F32
        ).astype(BF16)
        if d < n_xy:
            row_send[j] = rows
            row_copy(d).start()
        else:
            rows_in[c, me_xy] = rows

    loads[1].wait()
    send_weights(1)

    def forward_copy(d):
        place_xy = (me_xy + n_xy - d) % n_xy
        return pltpu.make_async_remote_copy(
            rows_in.at[c, place_xy], rows_in.at[c, place_xy], fwd_send_sem.at[d], fwd_recv_sem.at[d],
            device_id=(ep, et + 1 - 2 * c), device_id_type=MESH,
        )

    def forward_landing(d):
        place_xy = (me_xy + n_xy - d) % n_xy
        return pltpu.make_async_remote_copy(
            rows_in.at[1 - c, place_xy], rows_in.at[1 - c, place_xy], fwd_send_sem.at[d],
            fwd_recv_sem.at[d], device_id=(ep, et + 1 - 2 * c), device_id_type=MESH,
        )

    for d in range(n_xy):
        if d > 0:
            row_copy(d).wait_recv()
        forward_copy(d).start()

    loads[2].wait()
    send_weights(2)

    lane = lax.broadcasted_iota(jnp.int32, (tok, n_rows), 1).astype(F32)

    @pl.loop(0, NZ)
    def _(z):
        columns = idx_recv[z].T
        total = jnp.zeros((tok, n_rows), F32)
        for j in range(n_xy):
            at = columns[:, j : j + 1] + (j * line_rows + z * cap).astype(F32)
            total = jnp.where(at == lane, columns[:, n_xy + j : n_xy + j + 1], total)
        combine[z] = total.astype(BF16)

    for d in range(n_xy):
        forward_landing(d).wait_recv()

    n_part = part_send_sem.shape[1]
    part_rows = n_rows // n_part
    chunk_lines = n_xy // n_part
    block = own.shape[2]

    def product(k, b, q):
        total = jnp.zeros((part_rows, block), F32)
        for cc in range(2):
            left = rows_in[cc, pl.ds(q * chunk_lines, chunk_lines)].reshape(part_rows, width)
            right = gu_recv[k, b, pl.ds(cc * (n_ep // 4), n_ep // 4)].reshape(width, block)
            total = total + jnp.dot(left, right, preferred_element_type=F32)
        return total

    def part_copy(k, q):
        where = pl.ds(q * part_rows, part_rows)
        return pltpu.make_async_remote_copy(
            part_send.at[k, where], part_recv.at[k, where], part_send_sem.at[k, q], part_recv_sem.at[k, q],
            device_id=(ep, (et + 2) % 4), device_id_type=MESH,
        )

    for k in range(2):
        wait_weights(k)

        @pl.loop(0, n_part)
        def _(q):
            where = pl.ds(pl.multiple_of(q * part_rows, part_rows), part_rows)
            part_send[k, where] = product(k, 1 - h, q).astype(BF16)
            part_copy(k, q).start()

        @pl.loop(0, n_part)
        def _(q):
            where = pl.ds(pl.multiple_of(q * part_rows, part_rows), part_rows)
            own[k, where] = product(k, h, q)

    def hidden_copy(d, q):
        where = pl.ds(q * part_rows, part_rows)
        return pltpu.make_async_remote_copy(
            hid.at[et, where], hid.at[et, where], hid_send_sem.at[d, q], hid_recv_sem.at[d, q],
            device_id=(ep, (et + d) % 4), device_id_type=MESH,
        )

    @pl.loop(0, n_part)
    def _(q):
        where = pl.ds(pl.multiple_of(q * part_rows, part_rows), part_rows)
        part_copy(0, q).wait_recv()
        part_copy(1, q).wait_recv()
        g = own[0, where] + part_recv[0, where].astype(F32)
        u = own[1, where] + part_recv[1, where].astype(F32)
        hid[et, where] = (g / (1.0 + jnp.exp(-g)) * u).astype(BF16)
        for d in range(1, 4):
            hidden_copy(d, q).start()

    wait_weights(2)

    def out_copy(i, d):
        return pltpu.make_async_remote_copy(
            out_send.at[i], ret.at[me_xy], out_send_sem.at[d], ret_recv_sem.at[d],
            device_id=(i * NZ + me_z, et), device_id_type=MESH,
        )

    def down_chunk(q):
        for d in range(1, 4):
            hidden_copy(d, q).wait_recv()
        where = pl.ds(pl.multiple_of(q * part_rows, part_rows), part_rows)
        total = jnp.zeros((part_rows, width), F32)
        for k in range(4):
            right = down_recv[k].reshape(width, block)
            total = total + lax.dot_general(
                hid[k, where], right, (((1,), (1,)), ((), ())), preferred_element_type=F32
            )
        total = total.astype(BF16)
        for v in range(chunk_lines):
            i = q * chunk_lines + v
            rows = total[v * line_rows : (v + 1) * line_rows]
            d = (i - me_xy + n_xy) % n_xy

            @pl.when(d == 0)
            def _():
                ret[me_xy] = rows

            @pl.when(d != 0)
            def _():
                out_send[i] = rows
                out_copy(i, d).start()

    @pl.loop(0, n_part)
    def _(q):
        down_chunk(q)

    for d in range(1, n_xy):
        out_copy((me_xy + d) % n_xy, d).wait_recv()

    def sum_copy(d):
        peer_z = (me_z + d) % NZ
        return pltpu.make_async_remote_copy(
            zsend.at[peer_z], zrecv.at[me_z], z_send_sem.at[d], z_recv_sem.at[d],
            device_id=(me_xy * NZ + peer_z, et), device_id_type=MESH,
        )

    @pl.loop(1, NZ + 1)
    def _(d):
        z = (me_z + d) % NZ
        total = jnp.dot(
            combine[z], ret[...].reshape(n_rows, width), preferred_element_type=F32
        ).astype(BF16)

        @pl.when(d < NZ)
        def _():
            zsend[z] = total
            sum_copy(d).start()

        @pl.when(d == NZ)
        def _():
            zrecv[me_z] = total

    for d in range(1, NZ):
        sum_copy(d).wait_recv()
    result = zrecv[0].astype(F32)
    for z in range(1, NZ):
        result = result + zrecv[z].astype(F32)
    out_ref[...] = result.astype(BF16)

    for d in range(1, NZ):
        index_copy(d).wait_send()
        token_copy(d).wait_send()
        sum_copy(d).wait_send()
    for d in range(1, n_xy):
        row_copy(d).wait_send()
        out_copy((me_xy + d) % n_xy, d).wait_send()
    for d in range(n_xy):
        forward_copy(d).wait_send()
    for k in range(3):
        wait_weights_sent(k)

    @pl.loop(0, n_part)
    def _(q):
        for k in range(2):
            part_copy(k, q).wait_send()
        for d in range(1, 4):
            hidden_copy(d, q).wait_send()


def per_device(
    tokens, slot_ids, gate_weights, old_expert, new_expert, gate_proj, up_proj, down_proj
):
    n_ep = lax.axis_size("ep")
    n_xy = n_ep // NZ
    tok, width = tokens.shape
    top = slot_ids.shape[1]
    slots, depth, block = gate_proj.shape
    cap = min(tok, (tok * top * 5 + 4 * n_ep - 1) // (4 * n_ep))
    slot_index = jnp.arange(slots, dtype=jnp.int32)
    holders = new_expert[:, None] == old_expert[None, :]
    source = jnp.min(jnp.where(holders, slot_index[None, :], slots - 1), axis=1).astype(jnp.int32)
    line_rows = NZ * cap
    n_rows = n_xy * line_rows
    n_part = 4
    dma = pltpu.SemaphoreType.DMA
    scratch = [
        pltpu.VMEM((slots, depth, block), BF16),
        pltpu.VMEM((slots, depth, block), BF16),
        pltpu.VMEM((slots, depth, block), BF16),
        pltpu.VMEM((3, slots, depth, block), BF16),
        pltpu.VMEM((2, 2, n_ep // 2, depth, block), BF16),
        pltpu.VMEM((4, n_ep // 4, depth, block), BF16),
        pltpu.VMEM((NZ, 2 * n_xy, tok), F32),
        pltpu.VMEM((NZ, 2 * n_xy, tok), F32),
        pltpu.VMEM((NZ, tok, width), BF16),
        pltpu.VMEM((line_rows, NZ * tok), BF16),
        pltpu.VMEM((NZ, tok, n_rows), BF16),
        pltpu.VMEM((n_xy, line_rows, width), BF16),
        pltpu.VMEM((2, n_xy, line_rows, width), BF16),
        pltpu.VMEM((2, n_rows, block), BF16),
        pltpu.VMEM((2, n_rows, block), BF16),
        pltpu.VMEM((2, n_rows, block), F32),
        pltpu.VMEM((4, n_rows, block), BF16),
        pltpu.VMEM((n_xy, line_rows, width), BF16),
        pltpu.VMEM((n_xy, line_rows, width), BF16),
        pltpu.VMEM((NZ, tok, width), BF16),
        pltpu.VMEM((NZ, tok, width), BF16),
        dma((4,)), dma((3,)), dma((3,)), dma((1,)), dma((NZ,)), dma((NZ,)), dma((NZ,)), dma((NZ,)),
        dma((n_xy,)), dma((n_xy,)), dma((n_xy,)), dma((n_xy,)), dma((2, n_part)), dma((2, n_part)),
        dma((4, n_part)), dma((4, n_part)), dma((n_xy,)), dma((n_xy,)), dma((NZ,)), dma((NZ,)),
    ]
    vmem = pl.BlockSpec(memory_space=pltpu.VMEM)
    hbm = pl.BlockSpec(memory_space=pl.ANY)
    return pl.pallas_call(
        functools.partial(layer_kernel, cap),
        out_shape=jax.ShapeDtypeStruct((tok, width), BF16),
        in_specs=[pl.BlockSpec(memory_space=pltpu.SMEM), hbm, vmem, vmem, hbm, hbm, hbm],
        out_specs=vmem,
        scratch_shapes=scratch,
        compiler_params=pltpu.CompilerParams(
            collective_id=0, has_side_effects=True, vmem_limit_bytes=60 * 1024 * 1024
        ),
        name="moe_layer",
    )(source, tokens, slot_ids.T, gate_weights.T, gate_proj, up_proj, down_proj)


def solution(mesh):
    placed = (
        P("ep", "et"), P("ep", None), P("ep", None), P(), P(),
        P(None, "ep", "et"), P(None, "ep", "et"), P(None, "ep", "et"),
    )
    return jax.shard_map(
        per_device, mesh=mesh, in_specs=placed, out_specs=P("ep", "et"), check_vma=False
    )
```

time: 692 us -> 339 us (0.49)
  Pallas kernels: 0 us -> 334 us
  blocking collectives: 332 us -> 0 us
  waiting for transfers between devices: 176 us -> 0 us
  local copies, waits for them, and re-layouts: 83.3 us -> 1.65 us
  other arithmetic: 38.2 us -> 1.37 us
  starting transfers between devices: 25.8 us -> 0 us
  matrix products: 21.5 us -> 0 us
  between operations: 13.6 us -> 0.01 us
    pallas_call x0 -> x1, Pallas kernels: none -> 334 us  [per_device(): pl.pallas_call(functools.partial(layer_kernel, cap), out_shape=jax.ShapeD...]
    all_to_all x2 -> x0, blocking collectives: 319 us -> none  [the longest x1 258 us: per_device(): lax.all_to_all(gather_rows(full_rows, row_table, slot_total, capacity), '...]
    all_to_all x3 -> x0, waiting for transfers between devices: 93.5 us -> none  [the longest x1 66.7 us: per_device(): lax.all_to_all(expert_out.reshape(slot_total, capacity, -1).astype(jnp.bf...]
    unnamed x2 -> x0, waiting for transfers between devices: 82.6 us -> none
    gather x6 -> x0, local copies, waits for them, and re-layouts: 37 us -> none  [the longest x2 21.1 us: gather_rows(): jnp.take(padded, row_table, axis=0)]
    all_to_all x3 -> x0, starting transfers between devices: 25.6 us -> none  [the longest x1 12.9 us: per_device(): lax.all_to_all(expert_out.reshape(slot_total, capacity, -1).astype(jnp.bf...]
    dot_general x2 -> x0, matrix products: 21.5 us -> none  [the longest x1 15.3 us: per_device(): lax.dot_general(hidden, down_slab, (((1,), (1,)), ((), ())), preferred_el...]
    reshape x3 -> x0, local copies, waits for them, and re-layouts: 18.4 us -> none  [the longest x1 13.3 us: per_device(): rows_in = arrived.reshape(-1, arrived.shape[-1])]
  transfers between devices with their start and end apart: 4 -> 0, of which waited for: 3 -> 0; matrix products, arithmetic and copies ran while one was open for 11% -> 0% of each run, Pallas kernels for 0% -> 0%
where the time goes in v1:
time: 339 us; the launch traced here: 337 us
  Pallas kernels  334 us (99%)
    pallas_call x1, Pallas kernels, per_device(): pl.pallas_call(functools.partial(layer_kernel, cap), out_shape=jax.ShapeD...  334 us

profile of v1, /device:TPU:56, one launch (start us, length us, event | category | flops | bytes accessed | tf_op | source)
XLA Modules:
  0.0 336.9 jit_solution(601166920686896764)
XLA Ops:
  0.0 1.4 select_reduce_fusion.source_ref
  1.4 333.9 %moe_layer.1 = bf16[128,896]{1,0:T(8,128)(2,1)} custom-call(s32[64]{0:T(128)} %select_reduce_fusion.source_ref, bf16[128,896]{1,0:T(8,128)(2,1)} %tokens_hbm.1, s32[8,128]{1,0:T(8,128)} %bitcast.2, f32[8,128]{1,0:T(8,128)} %bitcast.3, bf16[64,56,256]{2,1,0:T(8,128)(2,1)} %gate_hbm.1, bf16[64,56,256]{2,1,0:T(8,128)(2,1)} %up_hbm.1, bf16[64,56,256]{2,1,0:T(8,128)(2,1)} %down_hbm.1), custom_call_target="tpu_custom_call" | custom-call | tf_op jit(solution)/shard_map/moe_layer/pallas_call | solution.py:414
  335.3 1.6 copy.10

commit v2 on v1

v2 whole, which is shorter than its diff:
```python
import functools

import jax
import jax.numpy as jnp
from jax import lax
from jax.experimental import pallas as pl
from jax.experimental.pallas import tpu as pltpu
from jax.sharding import PartitionSpec as P

MESH = pl.DeviceIdType.MESH
NZ = 8
EARLY = 0
LATE = 0
F32 = jnp.float32
BF16 = jnp.bfloat16


def layer_kernel(
    cap, features,
    source_ref, tokens_hbm, slot_t_ref, gate_t_ref, gate_hbm, up_hbm, down_hbm, out_ref,
    stage_gate, stage_up, stage_down, wsend, gu_recv, down_recv, idx_send, idx_recv, tok_all, pick, combine,
    row_send, rows_in, hid, out_send, ret, ring_send, ring_recv,
    load_sem, wsend_sem, wrecv_sem, tok_send_sem, tok_recv_sem, idx_send_sem, idx_recv_sem,
    row_send_sem, row_recv_sem, fwd_send_sem, fwd_recv_sem,
    hid_send_sem, hid_recv_sem, out_send_sem, ret_recv_sem, ring_send_sem, ring_recv_sem,
):
    n_ep = stage_gate.shape[0]
    n_xy = n_ep // NZ
    tok = tok_all.shape[1]
    width = tok_all.shape[2]
    line_rows = NZ * cap
    n_rows = n_xy * line_rows
    ep = lax.axis_index("ep")
    et = lax.axis_index("et")
    me_xy, me_z = ep // NZ, ep % NZ
    h, c = et // 2, et % 2
    x_half = me_xy // (n_xy // 2)
    sibling = et + 1 - 2 * c
    across = (et + 2) % 4
    quarter = ep // (n_ep // 4)
    weights_hbm = (gate_hbm, up_hbm, down_hbm)
    stage = (stage_gate, stage_up, stage_down)

    loads = [
        pltpu.make_async_copy(weights_hbm[k], stage[k], load_sem.at[k]) for k in range(3)
    ]
    token_load = pltpu.make_async_copy(tokens_hbm, tok_all.at[me_z], load_sem.at[3])
    token_load.start()
    for load in loads:
        load.start()

    barrier = pltpu.get_barrier_semaphore()

    def greet(other_ep, other_et):
        pl.semaphore_signal(barrier, inc=1, device_id=(other_ep, other_et), device_id_type=MESH)

    @pl.loop(1, n_ep)
    def _(k):
        greet((ep + k) % n_ep, et)

    @pl.loop(0, n_ep)
    def _(k):
        other_ep, other_et = et * (n_ep // 4) + k // 4, k % 4

        @pl.when(jnp.logical_or(other_ep != ep, other_et != et))
        def _():
            greet(other_ep, other_et)

    for v in range(n_xy // 2):
        greet(((1 - x_half) * (n_xy // 2) + v) * NZ + me_z, across)
    for d in range(1, 4):
        greet(ep, (et + d) % 4)

    row = lax.broadcasted_iota(jnp.int32, (n_ep, tok), 0)
    row_slot = (row % n_xy) * NZ + row // n_xy
    named = jnp.zeros((n_ep, tok), F32)
    weight = jnp.zeros((n_ep, tok), F32)
    for k in range(slot_t_ref.shape[0]):
        hit = slot_t_ref[k : k + 1, :] == row_slot
        named = jnp.where(hit, 1.0, named)
        weight = jnp.where(hit, gate_t_ref[k : k + 1, :], weight)
    earlier = (
        lax.broadcasted_iota(jnp.int32, (tok, tok), 0) < lax.broadcasted_iota(jnp.int32, (tok, tok), 1)
    )
    place = jnp.dot(
        named.astype(BF16), jnp.where(earlier, 1.0, 0.0).astype(BF16), preferred_element_type=F32
    )
    place = jnp.where(named > 0.5, place, -100000.0)
    for z in range(NZ):
        idx_send[z, 0:n_xy, :] = place[z * n_xy : (z + 1) * n_xy]
        idx_send[z, n_xy : 2 * n_xy, :] = weight[z * n_xy : (z + 1) * n_xy]
    idx_recv[me_z] = idx_send[me_z]
    token_load.wait()

    same_down = jnp.where(quarter == et, 1, 0)
    pl.semaphore_wait(barrier, (n_ep - 1) + (n_ep - same_down) + n_xy // 2 + 3)

    half_tok = tok // 2
    far = NZ // 2

    def token_copy(way, s):
        owner = (me_z - way * (s - 1)) % NZ
        start, size = (0, tok) if s < far else ((0, half_tok) if way > 0 else (half_tok, half_tok))
        side = 0 if way > 0 else 1
        rows = tok_all.at[owner, pl.ds(start, size)]
        return pltpu.make_async_remote_copy(
            rows, rows, tok_send_sem.at[side, s], tok_recv_sem.at[side, s],
            device_id=(me_xy * NZ + (me_z + way) % NZ, et), device_id_type=MESH,
        )

    def index_copy(d):
        peer_z = (me_z + d) % NZ
        return pltpu.make_async_remote_copy(
            idx_send.at[peer_z], idx_recv.at[me_z], idx_send_sem.at[d], idx_recv_sem.at[d],
            device_id=(me_xy * NZ + peer_z, et), device_id_type=MESH,
        )

    for way in (1, -1):
        token_copy(way, 1).start()
    for d in range(1, NZ):
        index_copy(d).start()

    def weight_target(k):
        if k < 2:
            return et, gu_recv.at[k, ep]
        return quarter, down_recv.at[et, ep % (n_ep // 4)]

    def send_weights(k, first, last):
        target_et, target = weight_target(k)

        @pl.loop(first, last)
        def _(m):
            far_m = m - n_xy
            d_xy = jnp.where(m < n_xy, m, far_m % n_xy)
            d_z = jnp.where(m < n_xy, 0, 1 + far_m % (NZ - 1))
            slot = ((me_xy + d_xy) % n_xy) * NZ + (me_z + d_z) % NZ
            wsend[k, slot] = stage[k][source_ref[slot]]

            @pl.when(jnp.logical_or(slot != ep, target_et != et))
            def _():
                pltpu.make_async_remote_copy(
                    wsend.at[k, slot], target, wsend_sem.at[k], wrecv_sem.at[k],
                    device_id=(slot, target_et), device_id_type=MESH,
                ).start()

            @pl.when(jnp.logical_and(slot == ep, target_et == et))
            def _():
                pltpu.make_async_copy(wsend.at[k, slot], target, wrecv_sem.at[k]).start()

    def wait_weights(k):
        landed = gu_recv.at[k] if k < 2 else down_recv
        pltpu.make_async_copy(landed, landed, wrecv_sem.at[k]).wait()

    def wait_weights_sent(k):
        target_et, target = weight_target(k)

        @pl.loop(0, n_ep)
        def _(slot):
            @pl.when(jnp.logical_or(slot != ep, target_et != et))
            def _():
                pltpu.make_async_remote_copy(
                    wsend.at[k, slot], target, wsend_sem.at[k], wrecv_sem.at[k],
                    device_id=(slot, target_et), device_id_type=MESH,
                ).wait_send()

    low = 16
    rest = cap - low
    low_rows, rest_rows = NZ * low, NZ * rest
    row_low = lax.broadcasted_iota(jnp.int32, (low, tok), 0).astype(F32)
    row_rest = lax.broadcasted_iota(jnp.int32, (rest_rows, tok), 0).astype(F32)

    def low_part(z):
        places = idx_recv[z]
        picked = jnp.concatenate(
            [jnp.where(places[j : j + 1, :] == row_low, 1.0, 0.0) for j in range(n_xy)], axis=0
        ).astype(BF16)
        rows = jnp.dot(picked, tok_all[z], preferred_element_type=F32).astype(BF16)
        where = pl.ds(pl.multiple_of(z * low, low), low)
        for j in range(n_xy):
            row_send[j, where] = rows[j * low : (j + 1) * low]

    def rest_part():
        for z in range(NZ):
            places = idx_recv[z]
            at = jnp.where(places >= float(low), places + float(z * rest - low), -1.0)
            pick[:, z * tok : (z + 1) * tok] = jnp.concatenate(
                [jnp.where(at[j : j + 1, :] == row_rest, 1.0, 0.0) for j in range(n_xy)], axis=0
            ).astype(BF16)
        rows = jnp.dot(
            pick[...], tok_all[...].reshape(NZ * tok, width), preferred_element_type=F32
        ).astype(BF16)
        for j in range(n_xy):
            row_send[j, low_rows:line_rows] = rows[j * rest_rows : (j + 1) * rest_rows]

    for k in range(3):
        loads[k].wait()
        send_weights(k, 0, n_xy)
    send_weights(0, n_xy, n_xy + EARLY)
    low_part(me_z)
    for d in range(1, NZ):
        index_copy(d).wait_recv()
    for s in range(1, far + 1):
        for way in (1, -1):
            token_copy(way, s).wait_recv()
            if s < far:
                token_copy(way, s + 1).start()
        if s < far:
            send_weights(0, n_xy + s * EARLY, n_xy + (s + 1) * EARLY)
            low_part((me_z - s) % NZ)
            low_part((me_z + s) % NZ)
        else:
            send_weights(0, n_xy + far * EARLY, n_xy + far * EARLY + LATE)
            low_part((me_z + far) % NZ)
    rest_part()

    def row_copy(d):
        peer_xy = (me_xy + d) % n_xy
        same_x = x_half == peer_xy // (n_xy // 2)
        return pltpu.make_async_remote_copy(
            row_send.at[peer_xy], rows_in.at[et, me_xy], row_send_sem.at[d], row_recv_sem.at[d],
            device_id=(peer_xy * NZ + me_z, jnp.where(same_x, et, across)), device_id_type=MESH,
        )

    for d in range(1, n_xy):
        row_copy(d).start()
    rows_in[et, me_xy] = row_send[me_xy]
    send_weights(0, n_xy + far * EARLY + LATE, n_ep)

    send_weights(1, n_xy, n_ep)
    send_weights(2, n_xy, n_ep)

    def pass_copy(step, d):
        place_xy = (me_xy + n_xy - d) % n_xy
        same_x = x_half == place_xy // (n_xy // 2)
        near, other = jnp.where(same_x, et, across), jnp.where(same_x, across, et)
        rows = rows_in.at[other if step == 2 else near, place_xy]
        return pltpu.make_async_remote_copy(
            rows, rows, fwd_send_sem.at[step, d], fwd_recv_sem.at[step, d],
            device_id=(ep, across if step == 0 else sibling), device_id_type=MESH,
        )

    for d in range(n_xy):
        if d > 0:
            row_copy(d).wait_recv()
        pass_copy(0, d).start()
        pass_copy(1, d).start()

    lane = lax.broadcasted_iota(jnp.int32, (tok, 128), 1).astype(F32)

    @pl.loop(0, NZ)
    def _(z):
        table = idx_recv[z].T
        places, weights = table[:, 0:n_xy], table[:, n_xy : 2 * n_xy]
        at_rest = jnp.where(places >= float(low), places + (z * rest - low).astype(F32), -100000.0)
        at_low = jnp.where(places < float(low), places, -100000.0)
        per_tile = 128 // rest_rows
        total = jnp.zeros((tok, 128), F32)
        for j in range(n_xy):
            total = jnp.where(at_low[:, j : j + 1] + float(j * low) == lane, weights[:, j : j + 1], total)
        combine[z, :, 0:128] = total.astype(BF16)
        for tile in range(n_xy // per_tile):
            total = jnp.zeros((tok, 128), F32)
            for v in range(per_tile):
                j = tile * per_tile + v
                total = jnp.where(
                    at_rest[:, j : j + 1] + float(v * rest_rows) == lane, weights[:, j : j + 1], total
                )
            combine[z, :, (tile + 1) * 128 : (tile + 2) * 128] = total.astype(BF16)

    for d in range(n_xy):
        pass_copy(0, d).wait_recv()
        pass_copy(2, d).start()
    for d in range(n_xy):
        pass_copy(1, d).wait_recv()
        pass_copy(2, d).wait_recv()

    n_part = hid_send_sem.shape[1]
    part_rows = n_rows // n_part
    chunk_lines = n_xy // n_part
    block = hid.shape[2]

    def product(k, q):
        total = jnp.zeros((part_rows, block), F32)
        for v in range(4):
            left = rows_in[v, pl.ds(q * chunk_lines, chunk_lines)].reshape(part_rows, width)
            right = gu_recv[k, pl.ds(v * (n_ep // 4), n_ep // 4)].reshape(width, block)
            total = total + jnp.dot(left, right, preferred_element_type=F32)
        return total

    def hidden_copy(step, q):
        where = pl.ds(q * part_rows, part_rows)
        rows = hid.at[across if step == 2 else et, where]
        return pltpu.make_async_remote_copy(
            rows, rows, hid_send_sem.at[step, q], hid_recv_sem.at[step, q],
            device_id=(ep, across if step == 0 else sibling), device_id_type=MESH,
        )

    wait_weights(0)
    wait_weights(1)

    @pl.loop(0, n_part)
    def _(q):
        where = pl.ds(pl.multiple_of(q * part_rows, part_rows), part_rows)
        g = product(0, q)
        u = product(1, q)
        hid[et, where] = (g / (1.0 + jnp.exp(-g)) * u).astype(BF16)
        hidden_copy(0, q).start()
        hidden_copy(1, q).start()

    @pl.loop(0, n_part)
    def _(q):
        hidden_copy(0, q).wait_recv()
        hidden_copy(2, q).start()

    wait_weights(2)

    def out_copy(i, d, f):
        lanes = pl.ds(features[f][0], features[f][1])
        return pltpu.make_async_remote_copy(
            out_send.at[i, :, lanes], ret.at[me_xy, :, lanes], out_send_sem.at[d, f], ret_recv_sem.at[d, f],
            device_id=(i * NZ + me_z, et), device_id_type=MESH,
        )

    def down_chunk(q):
        hidden_copy(1, q).wait_recv()
        hidden_copy(2, q).wait_recv()
        where = pl.ds(pl.multiple_of(q * part_rows, part_rows), part_rows)
        total = jnp.zeros((part_rows, width), F32)
        for k in range(4):
            right = down_recv[k].reshape(width, block)
            total = total + lax.dot_general(
                hid[k, where], right, (((1,), (1,)), ((), ())), preferred_element_type=F32
            )
        total = total.astype(BF16)
        for v in range(chunk_lines):
            i = q * chunk_lines + v
            rows = total[v * line_rows : (v + 1) * line_rows]
            d = (i - me_xy + n_xy) % n_xy

            @pl.when(d == 0)
            def _():
                ret[me_xy] = rows

            @pl.when(d != 0)
            def _():
                out_send[i] = rows
                out_copy(i, d, 0).start()

    @pl.loop(0, n_part)
    def _(q):
        down_chunk(q)

    for f in range(1, len(features)):
        for d in range(1, n_xy):
            out_copy((me_xy + d) % n_xy, d, f).start()

    def line_sum(z, f):
        lanes = pl.ds(features[f][0], features[f][1])
        where = pl.ds(pl.multiple_of(z * low, low), low)
        near = ret[:, where, lanes].reshape(n_xy * low, features[f][1])
        others = ret[:, low_rows:line_rows, lanes].reshape(n_xy * rest_rows, features[f][1])
        total = jnp.dot(combine[z, :, 0:128], near, preferred_element_type=F32)
        return total + jnp.dot(combine[z, :, 128:], others, preferred_element_type=F32)

    def sum_copy(way, k, f):
        side = 0 if way > 0 else 1
        start, size = (0, tok) if k < far else ((0, half_tok) if way > 0 else (half_tok, half_tok))
        lanes = pl.ds(features[f][0], features[f][1])
        return pltpu.make_async_remote_copy(
            ring_send.at[side, k - 1, pl.ds(start, size), lanes],
            ring_recv.at[side, k - 1, pl.ds(start, size), lanes],
            ring_send_sem.at[side, k - 1, f], ring_recv_sem.at[side, k - 1, f],
            device_id=(me_xy * NZ + (me_z + way) % NZ, et), device_id_type=MESH,
        )

    def ring_step(k, f):
        lanes = pl.ds(features[f][0], features[f][1])
        if k == far:
            if f == 0 or len(features) > 1:
                for d in range(1, n_xy):
                    out_copy((me_xy + d) % n_xy, d, f).wait_recv()
            total = line_sum((me_z + far) % NZ, f).astype(BF16)
            for side, way in ((0, 1), (1, -1)):
                start = side * half_tok
                ring_send[side, k - 1, start : start + half_tok, lanes] = total[start : start + half_tok]
                sum_copy(way, k, f).start()
            return
        for side, way in ((0, 1), (1, -1)):
            total = line_sum((me_z + way * k) % NZ, f)
            sum_copy(way, k + 1, f).wait_recv()
            if k + 1 == far:
                start = side * half_tok
                other = half_tok - start
                ring_send[side, k - 1, start : start + half_tok, lanes] = (
                    total[start : start + half_tok]
                    + ring_recv[side, k, start : start + half_tok, lanes].astype(F32)
                ).astype(BF16)
                ring_send[side, k - 1, other : other + half_tok, lanes] = total[
                    other : other + half_tok
                ].astype(BF16)
            else:
                ring_send[side, k - 1, :, lanes] = (
                    total + ring_recv[side, k, :, lanes].astype(F32)
                ).astype(BF16)
            sum_copy(way, k, f).start()

    def finish(f):
        lanes = pl.ds(features[f][0], features[f][1])
        total = line_sum(me_z, f)
        for side, way in ((0, 1), (1, -1)):
            sum_copy(way, 1, f).wait_recv()
            total = total + ring_recv[side, 0, :, lanes].astype(F32)
        out_ref[:, lanes] = total.astype(BF16)

    lag = 2
    for t in range(far + lag * (len(features) - 1) + 1):
        for f in range(len(features)):
            s = t - lag * f
            if 0 <= s < far:
                ring_step(far - s, f)
            elif s == far:
                finish(f)

    for d in range(1, NZ):
        index_copy(d).wait_send()
    for way in (1, -1):
        for s in range(1, far + 1):
            token_copy(way, s).wait_send()
            for f in range(len(features)):
                sum_copy(way, s, f).wait_send()
    for d in range(1, n_xy):
        row_copy(d).wait_send()
        for f in range(len(features)):
            out_copy((me_xy + d) % n_xy, d, f).wait_send()
    for d in range(n_xy):
        for step in range(3):
            pass_copy(step, d).wait_send()
    for k in range(3):
        wait_weights_sent(k)

    @pl.loop(0, n_part)
    def _(q):
        for step in range(3):
            hidden_copy(step, q).wait_send()


def per_device(
    tokens, slot_ids, gate_weights, old_expert, new_expert, gate_proj, up_proj, down_proj
):
    n_ep = lax.axis_size("ep")
    n_xy = n_ep // NZ
    tok, width = tokens.shape
    top = slot_ids.shape[1]
    slots, depth, block = gate_proj.shape
    cap = min(tok, (tok * top * 5 + 4 * n_ep - 1) // (4 * n_ep))
    slot_index = jnp.arange(slots, dtype=jnp.int32)
    holders = new_expert[:, None] == old_expert[None, :]
    source = jnp.min(jnp.where(holders, slot_index[None, :], slots - 1), axis=1).astype(jnp.int32)
    line_rows = NZ * cap
    n_rows = n_xy * line_rows
    n_part = 4
    features = ((0, 512), (512, width - 512))
    n_feat = len(features)
    dma = pltpu.SemaphoreType.DMA
    scratch = [
        pltpu.VMEM((slots, depth, block), BF16),
        pltpu.VMEM((slots, depth, block), BF16),
        pltpu.VMEM((slots, depth, block), BF16),
        pltpu.VMEM((3, slots, depth, block), BF16),
        pltpu.VMEM((2, n_ep, depth, block), BF16),
        pltpu.VMEM((4, n_ep // 4, depth, block), BF16),
        pltpu.VMEM((NZ, 2 * n_xy, tok), F32),
        pltpu.VMEM((NZ, 2 * n_xy, tok), F32),
        pltpu.VMEM((NZ, tok, width), BF16),
        pltpu.VMEM((n_xy * NZ * (cap - 16), NZ * tok), BF16),
        pltpu.VMEM((NZ, tok, n_xy * (16 + NZ * (cap - 16))), BF16),
        pltpu.VMEM((n_xy, line_rows, width), BF16),
        pltpu.VMEM((4, n_xy, line_rows, width), BF16),
        pltpu.VMEM((4, n_rows, block), BF16),
        pltpu.VMEM((n_xy, line_rows, width), BF16),
        pltpu.VMEM((n_xy, line_rows, width), BF16),
        pltpu.VMEM((2, NZ // 2, tok, width), BF16),
        pltpu.VMEM((2, NZ // 2, tok, width), BF16),
        dma((4,)), dma((3,)), dma((3,)), dma((2, NZ // 2 + 1)), dma((2, NZ // 2 + 1)), dma((NZ,)), dma((NZ,)),
        dma((n_xy,)), dma((n_xy,)), dma((3, n_xy)), dma((3, n_xy)),
        dma((3, n_part)), dma((3, n_part)), dma((n_xy, n_feat)), dma((n_xy, n_feat)),
        dma((2, NZ // 2, n_feat)), dma((2, NZ // 2, n_feat)),
    ]
    vmem = pl.BlockSpec(memory_space=pltpu.VMEM)
    hbm = pl.BlockSpec(memory_space=pl.ANY)
    return pl.pallas_call(
        functools.partial(layer_kernel, cap, features),
        out_shape=jax.ShapeDtypeStruct((tok, width), BF16),
        in_specs=[pl.BlockSpec(memory_space=pltpu.SMEM), hbm, vmem, vmem, hbm, hbm, hbm],
        out_specs=vmem,
        scratch_shapes=scratch,
        compiler_params=pltpu.CompilerParams(
            collective_id=0, has_side_effects=True, vmem_limit_bytes=60 * 1024 * 1024
        ),
        name="moe_layer",
    )(source, tokens, slot_ids.T, gate_weights.T, gate_proj, up_proj, down_proj)


def solution(mesh):
    placed = (
        P("ep", "et"), P("ep", None), P("ep", None), P(), P(),
        P(None, "ep", "et"), P(None, "ep", "et"), P(None, "ep", "et"),
    )
    return jax.shard_map(
        per_device, mesh=mesh, in_specs=placed, out_specs=P("ep", "et"), check_vma=False
    )
```

time: 339 us -> 229 us (0.68)
  Pallas kernels: 334 us -> 223 us
    pallas_call x1, Pallas kernels: 334 us -> 223 us  [per_device(): pl.pallas_call(functools.partial(layer_kernel, cap, features), out_shape=...]
where the time goes in v2:
time: 229 us; the launch traced here: 226 us
  Pallas kernels  223 us (97%)
    pallas_call x1, Pallas kernels, per_device(): pl.pallas_call(functools.partial(layer_kernel, cap, features), out_shape=...  223 us

profile of v2, /device:TPU:56, one launch (start us, length us, event | category | flops | bytes accessed | tf_op | source)
XLA Modules:
  0.0 226.4 jit_solution(12880716631478970052)
XLA Ops:
  0.0 1.4 select_reduce_fusion.source_ref
  1.4 223.4 %moe_layer.1 = bf16[128,896]{1,0:T(8,128)(2,1)} custom-call(s32[64]{0:T(128)} %select_reduce_fusion.source_ref, bf16[128,896]{1,0:T(8,128)(2,1)} %tokens_hbm.1, s32[8,128]{1,0:T(8,128)} %bitcast.2, f32[8,128]{1,0:T(8,128)} %bitcast.3, bf16[64,56,256]{2,1,0:T(8,128)(2,1)} %gate_hbm.1, bf16[64,56,256]{2,1,0:T(8,128)(2,1)} %up_hbm.1, bf16[64,56,256]{2,1,0:T(8,128)(2,1)} %down_hbm.1), custom_call_target="tpu_custom_call" | custom-call | tf_op jit(solution)/shard_map/moe_layer/pallas_call | solution.py:491
  224.8 1.6 copy.10

commit v3 on v2

--- a/solution.py
+++ b/solution.py
@@ -9,8 +9,7 @@
 
 MESH = pl.DeviceIdType.MESH
 NZ = 8
-EARLY = 0
-LATE = 0
+EARLY = 24
 F32 = jnp.float32
 BF16 = jnp.bfloat16
 
@@ -195,7 +194,6 @@
     for k in range(3):
         loads[k].wait()
         send_weights(k, 0, n_xy)
-    send_weights(0, n_xy, n_xy + EARLY)
     low_part(me_z)
     for d in range(1, NZ):
         index_copy(d).wait_recv()
@@ -204,13 +202,11 @@
             token_copy(way, s).wait_recv()
             if s < far:
                 token_copy(way, s + 1).start()
+        if s == far - 1:
+            send_weights(0, n_xy, n_xy + EARLY)
+        low_part((me_z + s) % NZ)
         if s < far:
-            send_weights(0, n_xy + s * EARLY, n_xy + (s + 1) * EARLY)
             low_part((me_z - s) % NZ)
-            low_part((me_z + s) % NZ)
-        else:
-            send_weights(0, n_xy + far * EARLY, n_xy + far * EARLY + LATE)
-            low_part((me_z + far) % NZ)
     rest_part()
 
     def row_copy(d):
@@ -224,7 +220,7 @@
     for d in range(1, n_xy):
         row_copy(d).start()
     rows_in[et, me_xy] = row_send[me_xy]
-    send_weights(0, n_xy + far * EARLY + LATE, n_ep)
+    send_weights(0, n_xy + EARLY, n_ep)
 
     send_weights(1, n_xy, n_ep)
     send_weights(2, n_xy, n_ep)

time: 229 us -> 224 us (0.978)
  Pallas kernels: 223 us -> 218 us
    pallas_call x1, Pallas kernels: 223 us -> 218 us  [per_device(): pl.pallas_call(functools.partial(layer_kernel, cap, features), out_shape=...]
where the time goes in v3:
time: 224 us; the launch traced here: 221 us
  Pallas kernels  218 us (97%)
    pallas_call x1, Pallas kernels, per_device(): pl.pallas_call(functools.partial(layer_kernel, cap, features), out_shape=...  218 us

profile of v3, /device:TPU:56, one launch (start us, length us, event | category | flops | bytes accessed | tf_op | source)
XLA Modules:
  0.0 220.9 jit_solution(13658278371429557130)
XLA Ops:
  0.0 1.4 select_reduce_fusion.source_ref
  1.4 217.9 %moe_layer.1 = bf16[128,896]{1,0:T(8,128)(2,1)} custom-call(s32[64]{0:T(128)} %select_reduce_fusion.source_ref, bf16[128,896]{1,0:T(8,128)(2,1)} %tokens_hbm.1, s32[8,128]{1,0:T(8,128)} %bitcast.2, f32[8,128]{1,0:T(8,128)} %bitcast.3, bf16[64,56,256]{2,1,0:T(8,128)(2,1)} %gate_hbm.1, bf16[64,56,256]{2,1,0:T(8,128)(2,1)} %up_hbm.1, bf16[64,56,256]{2,1,0:T(8,128)(2,1)} %down_hbm.1), custom_call_target="tpu_custom_call" | custom-call | tf_op jit(solution)/shard_map/moe_layer/pallas_call | solution.py:487
  219.3 1.6 copy.10

commit v4 on v3

--- a/solution.py
+++ b/solution.py
@@ -18,7 +18,7 @@
     cap, features,
     source_ref, tokens_hbm, slot_t_ref, gate_t_ref, gate_hbm, up_hbm, down_hbm, out_ref,
     stage_gate, stage_up, stage_down, wsend, gu_recv, down_recv, idx_send, idx_recv, tok_all, pick, combine,
-    row_send, rows_in, hid, out_send, ret, ring_send, ring_recv,
+    row_send, rows_in, hid, out_send, ret, rest_sum, ring_send, ring_recv,
     load_sem, wsend_sem, wrecv_sem, tok_send_sem, tok_recv_sem, idx_send_sem, idx_recv_sem,
     row_send_sem, row_recv_sem, fwd_send_sem, fwd_recv_sem,
     hid_send_sem, hid_recv_sem, out_send_sem, ret_recv_sem, ring_send_sem, ring_recv_sem,
@@ -354,9 +354,20 @@
         lanes = pl.ds(features[f][0], features[f][1])
         where = pl.ds(pl.multiple_of(z * low, low), low)
         near = ret[:, where, lanes].reshape(n_xy * low, features[f][1])
+        return rest_sum[z, :, lanes] + jnp.dot(
+            combine[z, :, 0:128], near, preferred_element_type=F32
+        )
+
+    def rest_sums(f):
+        lanes = pl.ds(features[f][0], features[f][1])
         others = ret[:, low_rows:line_rows, lanes].reshape(n_xy * rest_rows, features[f][1])
-        total = jnp.dot(combine[z, :, 0:128], near, preferred_element_type=F32)
-        return total + jnp.dot(combine[z, :, 128:], others, preferred_element_type=F32)
+
+        @pl.loop(0, 2)
+        def _(v):
+            zs = pl.ds(v * (NZ // 2), NZ // 2)
+            left = combine[zs, :, 128:].reshape(NZ // 2 * tok, n_xy * rest_rows)
+            total = jnp.dot(left, others, preferred_element_type=F32)
+            rest_sum[zs, :, lanes] = total.reshape(NZ // 2, tok, features[f][1])
 
     def sum_copy(way, k, f):
         side = 0 if way > 0 else 1
@@ -375,6 +386,7 @@
             if f == 0 or len(features) > 1:
                 for d in range(1, n_xy):
                     out_copy((me_xy + d) % n_xy, d, f).wait_recv()
+            rest_sums(f)
             total = line_sum((me_z + far) % NZ, f).astype(BF16)
             for side, way in ((0, 1), (1, -1)):
                 start = side * half_tok
@@ -475,6 +487,7 @@
         pltpu.VMEM((4, n_rows, block), BF16),
         pltpu.VMEM((n_xy, line_rows, width), BF16),
         pltpu.VMEM((n_xy, line_rows, width), BF16),
+        pltpu.VMEM((NZ, tok, width), F32),
         pltpu.VMEM((2, NZ // 2, tok, width), BF16),
         pltpu.VMEM((2, NZ // 2, tok, width), BF16),
         dma((4,)), dma((3,)), dma((3,)), dma((2, NZ // 2 + 1)), dma((2, NZ // 2 + 1)), dma((NZ,)), dma((NZ,)),

time: 224 us -> 224 us (level)
  no operation moved by 1% of the time
where the time goes in v4:
time: 224 us; the launch traced here: 221 us
  Pallas kernels  218 us (97%)
    pallas_call x1, Pallas kernels, per_device(): pl.pallas_call(functools.partial(layer_kernel, cap, features), out_shape=...  218 us

profile of v4, /device:TPU:56, one launch (start us, length us, event | category | flops | bytes accessed | tf_op | source)
XLA Modules:
  0.0 221.3 jit_solution(406956582498167409)
XLA Ops:
  0.0 1.4 select_reduce_fusion.source_ref
  1.4 218.3 %moe_layer.1 = bf16[128,896]{1,0:T(8,128)(2,1)} custom-call(s32[64]{0:T(128)} %select_reduce_fusion.source_ref, bf16[128,896]{1,0:T(8,128)(2,1)} %tokens_hbm.1, s32[8,128]{1,0:T(8,128)} %bitcast.2, f32[8,128]{1,0:T(8,128)} %bitcast.3, bf16[64,56,256]{2,1,0:T(8,128)(2,1)} %gate_hbm.1, bf16[64,56,256]{2,1,0:T(8,128)(2,1)} %up_hbm.1, bf16[64,56,256]{2,1,0:T(8,128)(2,1)} %down_hbm.1), custom_call_target="tpu_custom_call" | custom-call | tf_op jit(solution)/shard_map/moe_layer/pallas_call | solution.py:500
  219.7 1.6 copy.10
